TPU v7x, 256 devices: a whole 4x4x8 slice. The times are simulated.
256 devices in a mesh: quad: 8 (over x, z_hi), py: 8 (over y, core), pz: 4 (over z_lo).
Axes of the slice: x: 4, y: 4, z: 8 (z_hi: 2, z_lo: 4; z = z_hi * 4 + z_lo), core: 2. Of those that a mesh axis runs over, the one named last changes fastest.
Arguments:
- source_real: float32 [4, 16, 128, 512], P(None, None, 'py', 'pz'), may hold values from -6 to 6
- source_imag: float32 [4, 16, 128, 512], P(None, None, 'py', 'pz'), may hold values from -2 to 2
- potential: float32 [16, 128, 512], P(None, 'py', 'pz'), may hold values from 0 to 2
- center: float32 [1], replicated, may hold values from 4.5 to 6
- radius: float32 [1], replicated, may hold values from 1 to 2
Outputs:
- moments: float32 [4, 2, 4, 16, 128, 512], P(None, None, None, 'quad', 'py', 'pz')
All inputs are finite; a program needn't handle non-finite values.
Results may differ from a plain program's by a relative error of at most 0.0003.
Values sent between devices are 32-bit elements; how exact they have to be, the bound alone decides.
A program may use at most 128 MiB of HBM per device.

v0:
```python
import math
import jax
import jax.numpy as jnp
from jax import lax
from jax.sharding import PartitionSpec as P

QPTS = 8
MOMS = 4
stencil_weights = (-205.0 / 72.0, 8.0 / 5.0, -1.0 / 5.0, 8.0 / 315.0, -1.0 / 560.0)


def with_halo(value, sides, width):
    edges = {}
    for axis, dim in sides:
        count, length = (lax.axis_size(axis), value.shape[dim])
        up = [(i, (i + 1) % count) for i in range(count)]
        last = lax.slice_in_dim(value, length - width, length, axis=dim)
        initial = lax.slice_in_dim(value, 0, width, axis=dim)
        edges[dim] = (
            lax.ppermute(last, axis, up),
            lax.ppermute(initial, axis, [(b, a) for a, b in up]),
        )
    done = []
    for _, dim in sides:
        low, high = edges[dim]
        around = [(width, width) if d in done else (0, 0) for d in range(value.ndim)]
        value = jnp.concatenate([jnp.pad(low, around), value, jnp.pad(high, around)], axis=dim)
        done.append(dim)
    return value


def sent_to_all(value, axis):
    count = lax.axis_size(axis)
    return lax.all_to_all(
        jnp.broadcast_to(value[None], (count, *value.shape)), axis, 0, 0, tiled=True
    )


def over_copies(value, axis):
    return sent_to_all(value, axis).sum(axis=0)


def packed_total(arrays, axis):
    ends = [0]
    for a in arrays:
        ends.append(ends[-1] + a.size)
    running = over_copies(jnp.concatenate([a.ravel() for a in arrays]), axis)
    return tuple((running[b:e].reshape(a.shape) for a, b, e in zip(arrays, ends, ends[1:])))


def apply_operator(field, potential):
    padded = with_halo(field, (("py", 4), ("pz", 5)), 4)
    width_y = field.shape[4]
    width_z = field.shape[5]
    laplace = 3.0 * stencil_weights[0] * field
    for offset in range(1, 5):
        beside_all = jnp.roll(field, offset, 3) + jnp.roll(field, -offset, 3)
        beside_all = (
            beside_all + padded[:, :, :, :, 4 + offset : 4 + offset + width_y, 4 : 4 + width_z]
        )
        beside_all = (
            beside_all + padded[:, :, :, :, 4 - offset : 4 - offset + width_y, 4 : 4 + width_z]
        )
        beside_all = (
            beside_all + padded[:, :, :, :, 4 : 4 + width_y, 4 + offset : 4 + offset + width_z]
        )
        beside_all = (
            beside_all + padded[:, :, :, :, 4 : 4 + width_y, 4 - offset : 4 - offset + width_z]
        )
        laplace = laplace + stencil_weights[offset] * beside_all
    return -0.5 * laplace + potential * field


def complex_mul(left, right):
    return (left[0] * right[0] - left[1] * right[1], left[0] * right[1] + left[1] * right[0])


def complex_div(left, right):
    norm_sq = right[0] * right[0] + right[1] * right[1]
    return (
        (left[0] * right[0] + left[1] * right[1]) / norm_sq,
        (left[1] * right[0] - left[0] * right[1]) / norm_sq,
    )


def local_bilinear(left, right):
    both = complex_mul(left, right)
    return (jnp.sum(both[0], axis=(-3, -2, -1)), jnp.sum(both[1], axis=(-3, -2, -1)))


def spread(value):
    return (value[0][..., None, None, None], value[1][..., None, None, None])


def moment_terms(solution, angles, radius_value):
    orders = jnp.arange(1, MOMS + 1).astype(jnp.float32)
    phase = orders[:, None] * angles[None, :]
    weight_re = radius_value / QPTS * jnp.cos(phase)
    weight_im = radius_value / QPTS * jnp.sin(phase)
    highest = lax.Precision.HIGHEST
    real_part = jnp.einsum("kq,qsxyz->ksxyz", weight_re, solution[:, 0], precision=highest)
    real_part = real_part - jnp.einsum(
        "kq,qsxyz->ksxyz", weight_im, solution[:, 1], precision=highest
    )
    imag_part = jnp.einsum("kq,qsxyz->ksxyz", weight_re, solution[:, 1], precision=highest)
    imag_part = imag_part + jnp.einsum(
        "kq,qsxyz->ksxyz", weight_im, solution[:, 0], precision=highest
    )
    return jnp.stack([real_part, imag_part], 1)


def per_device(source_real, source_imag, potential, center, radius):
    groups = lax.axis_size("quad")
    local_count = QPTS // groups
    first_point = lax.axis_index("quad") * local_count
    indices = (first_point + jnp.arange(local_count)).astype(jnp.float32)
    angles = 2.0 * math.pi * (indices + 0.5) / QPTS
    shift_re = center[0] + radius[0] * jnp.cos(angles)
    shift_im = radius[0] * jnp.sin(angles)
    shift_pair = (shift_re[:, None], shift_im[:, None])
    shift_field = (shift_re[:, None, None, None, None], shift_im[:, None, None, None, None])
    source = (source_real, source_imag)
    applied = apply_operator(jnp.stack(source)[None], potential)[0]
    hsource = (applied[0], applied[1])
    rho_local = local_bilinear(source, source)
    curv_local = local_bilinear(source, hsource)
    totals = packed_total((rho_local[0], rho_local[1], curv_local[0], curv_local[1]), ("py", "pz"))
    rho_first = (totals[0], totals[1])
    curv_first = (totals[2], totals[3])
    scaled = complex_mul(shift_pair, rho_first)
    denom = (scaled[0] - curv_first[0], scaled[1] - curv_first[1])
    alpha_first = complex_div(rho_first, denom)
    alpha_wide = spread(alpha_first)
    first_iterate = complex_mul(alpha_wide, source)
    shifted = complex_mul(shift_field, source)
    image = (shifted[0] - hsource[0], shifted[1] - hsource[1])
    moved = complex_mul(alpha_wide, image)
    residual = (source[0] - moved[0], source[1] - moved[1])
    hres = apply_operator(jnp.stack(residual, 1), potential)
    shifted_res = complex_mul(shift_field, residual)
    image_res = (shifted_res[0] - hres[:, 0], shifted_res[1] - hres[:, 1])
    rho_part = local_bilinear(residual, residual)
    mixed_part = local_bilinear(residual, image_res)
    paired = packed_total((rho_part[0], rho_part[1], mixed_part[0], mixed_part[1]), ("py", "pz"))
    rho_next = (paired[0], paired[1])
    mixed = (paired[2], paired[3])
    beta = complex_div(rho_next, rho_first)
    carried = complex_mul(spread(beta), source)
    direction = (residual[0] + carried[0], residual[1] + carried[1])
    correction = complex_div(complex_mul(beta, rho_next), alpha_first)
    curv_next = (mixed[0] - correction[0], mixed[1] - correction[1])
    alpha_next = complex_div(rho_next, curv_next)
    step_part = complex_mul(spread(alpha_next), direction)
    solution = jnp.stack((first_iterate[0] + step_part[0], first_iterate[1] + step_part[1]), 1)
    gathered = lax.all_to_all(solution, "quad", split_axis=3, concat_axis=0, tiled=True)
    all_angles = 2.0 * math.pi * (jnp.arange(gathered.shape[0]).astype(jnp.float32) + 0.5) / QPTS
    return moment_terms(gathered, all_angles, radius[0])


def solution(mesh):
    in_specs = (P(None, None, "py", "pz"), P(None, None, "py", "pz"), P(None, "py", "pz"), P(), P())
    out_specs = P(None, None, None, "quad", "py", "pz")
    return jax.shard_map(
        per_device, mesh=mesh, in_specs=in_specs, out_specs=out_specs, check_vma=False
    )
```

profile of v0, /device:TPU:33, one launch (start us, length us, event | category | flops | bytes accessed | tf_op | source)
XLA Modules:
  0.0 176.5 jit_solution(8085165533482283820)
XLA Ops:
  0.0 1.3 pad_maximum_fusion.5
  1.6 0.9 fusion.89
  2.5 1.9 %collective-permute-start.1 = (f32[1,2,4,16,4,128]{5,3,4,2,1,0:T(8,128)}, f32[1,2,4,16,4,128]{5,3,4,2,1,0:T(8,128)S(1)}, u32[]{:S(2)}, u32[]{:S(2)}) collective-permute-start(f32[1,2,4,16,4,128]{5,3,4,2,1,0:T(8,128)} %get-tuple-element.79), channel_id=1, source_target_pairs={{0,4},{4,8},{8,12},{12,16},{16,20},{20,24},{24,28},{28,0},{1,5},{5... | collective-permute-start | bytes 786440 | tf_op jit(solution)/shard_map/ppermute | solution.py:20
  4.7 1.6 copy.158
  6.7 1.6 copy.160
  8.3 1.3 collective-permute-start.3
  11.4 1.3 copy.156
  12.7 1.3 copy.150
  14.0 1.2 copy.151
  15.3 1.2 copy.163
  16.5 1.2 copy.164
  17.7 1.2 copy.169
  18.9 1.2 copy.170
  20.1 1.1 copy.175
  21.2 1.1 copy.176
  26.5 1.8 copy.222
  28.3 1.8 copy.223
  30.1 1.1 copy.157
  31.2 3.6 %select_maximum_fusion.3 = (f32[1,2,4,16,24,132]{5,4,3,2,1,0:T(8,128)S(1)}, f32[1,2,4,16,24,132]{5,4,3,2,1,0:T(8,128)S(1)}) fusion(f32[1,2,4,16,16,4]{5,4,3,2,1,0:T(8,128)S(1)} %copy.222, f32[1,2,4,16,4,128]{5,4,3,2,1,0:T(4,128)S(1)} %copy.157, f32[1,2,4,16,16,128]{5,4,3,2,1,0:T(8,128)} %copy.156, f32[1,2,4,16,4,128]{5,4,3,2,1,0:T(4,128)S(1)} %copy.155, ...), kind=kLoop, calls=%fused_computation.45 | loop fusion | flops 4055040 | bytes 4882432 | tf_op jit(solution)/shard_map/concatenate | solution.py:27
  34.8 4.4 %fusion.6 = (f32[1,2,4,16,16,128]{5,3,4,2,1,0:T(8,128)}, f32[1,2,4,16,16,128]{5,3,4,2,1,0:T(8,128)}, f32[1,2,4,16,16,128]{5,3,4,2,1,0:T(8,128)}, f32[1,2,4,16,16...) fusion(f32[1,2,4,16,16,128]{5,3,4,2,1,0:T(8,128)S(1)} %bitcast., ...), kind=kLoop, calls=%fused_computation.69 | loop fusion | flops 2097152 | bytes 9961472 | tf_op jit(solution)/shard_map/concatenate | solution.py:27
  39.2 10.0 %fusion.23 = f32[1,2,4,16,16,128]{5,4,3,2,1,0:T(8,128)S(1)} fusion(f32[1,2,4,16,24,132]{5,4,3,2,1,0:T(8,128)S(1)} %get-tuple-element.26, f32[1,2,4,16,24,132]{5,4,3,2,1,0:T(8,128)S(1)} %get-tuple-element.25, f32[1,2,4,15,16,128]{5,4,3,2,1,0:T(8,128)} %copy.150, f32[1,2,4,1,16,128]{5,4,3,2,1,0:T(8,128)} %bitcast.138, f32[1,2,4,1,16,128]{5,4,3,2,1,0:T(8,128)} %bitcast.137, ...), kind=kLoop, calls=%fused_computation.103 | loop fusion | flops 10747904 | bytes 27394048 | tf_op jit(solution)/shard_map/add | solution.py:71
  50.3 11.2 %all-to-all-start = ((f32[32,1,16]{2,1,0:T(1,128)}), f32[32,1,16]{2,1,0:T(1,128)S(1)}, u32[]{:S(2)}, u32[]{:S(2)}) async-start(f32[32,1,16]{2,1,0:T(1,128)} %broadcast_in_dim.7), calls=%async_computation | async-start | bytes 32768 | tf_op jit(solution)/shard_map/all_to_all | solution.py:34
  63.0 4.6 %all-to-all-done = f32[32,1,16]{2,1,0:T(1,128)S(1)} async-done(((f32[32,1,16]{2,1,0:T(1,128)}), f32[32,1,16]{2,1,0:T(1,128)S(1)}, u32[]{:S(2)}, u32[]{:S(2)}) %all-to-all-start) | async-done | bytes 2080 | tf_op jit(solution)/shard_map/all_to_all | solution.py:34
  68.0 0.7 fusion.53
  68.8 0.8 fusion.55
  69.6 1.3 fusion.43
  71.6 1.5 fusion.41
  73.1 1.5 fusion.39
  74.7 1.3 fusion.8
  76.1 0.7 copy.214
  78.1 1.1 collective-permute-start.5
  79.3 2.8 %copy.216 = f32[1,2,4,16,16,4]{4,3,5,2,1,0:T(8,128)} copy(f32[1,2,4,16,16,4]{5,4,3,2,1,0:T(8,128)} %get-tuple-element.53) | data formatting | bytes 65536
  82.1 1.1 collective-permute-start.6
  83.2 1.6 copy.217
  85.1 1.4 fusion.45
  87.2 3.6 %collective-permute-done.6 = f32[1,2,4,16,16,4]{4,3,5,2,1,0:T(8,128)} collective-permute-done((f32[1,2,4,16,16,4]{4,3,5,2,1,0:T(8,128)}, f32[1,2,4,16,16,4]{4,3,5,2,1,0:T(8,128)}, u32[]{:S(2)}, u32[]{:S(2)}) %collective-permute-start.6) | collective-permute-done | bytes 32800 | tf_op jit(solution)/shard_map/ppermute | solution.py:21
  90.7 1.8 copy.224
  92.5 3.9 %collective-permute-done.7 = f32[1,2,4,16,16,4]{4,3,5,2,1,0:T(8,128)} collective-permute-done((f32[1,2,4,16,16,4]{4,3,5,2,1,0:T(8,128)}, f32[1,2,4,16,16,4]{4,3,5,2,1,0:T(8,128)}, u32[]{:S(2)}, u32[]{:S(2)}) %collective-permute-start.7) | collective-permute-done | bytes 32800 | tf_op jit(solution)/shard_map/ppermute | solution.py:20
  96.4 2.7 %copy.225 = f32[1,2,4,16,16,4]{5,4,3,2,1,0:T(8,128)} copy(f32[1,2,4,16,16,4]{4,3,5,2,1,0:T(8,128)} %collective-permute-done.7) | data formatting | bytes 65536
  99.1 1.1 copy.182
  100.3 1.1 copy.184
  101.7 4.0 %select_maximum_fusion.1 = (f32[1,2,4,16,24,132]{5,4,3,2,1,0:T(8,128)}, f32[1,2,4,16,24,132]{5,4,3,2,1,0:T(8,128)}) fusion(f32[1,2,4,16,16,4]{5,4,3,2,1,0:T(8,128)S(1)} %copy.224, f32[1,2,4,16,4,128]{5,4,3,2,1,0:T(4,128)S(1)} %copy.182, f32[1,1,4,16,16,128]{5,4,3,2,1,0:T(8,128)S(1)} %bitcast.126, f32[1,1,4,16,16,128]{5,4,3,2,1,0:T(8,128)S(1)} %bitcast.113, ...), kind=kLoop, calls=%fused_computation.42 | loop fusion | flops 4866048 | bytes 4882432 | tf_op jit(solution)/shard_map/concatenate | solution.py:27
  105.7 12.7 %fusion.13 = f32[1,2,4,16,16,128]{5,4,3,2,1,0:T(8,128)S(1)} fusion(f32[1,2,4,16,24,132]{5,4,3,2,1,0:T(8,128)} %get-tuple-element.24, f32[1,2,4,16,24,132]{5,4,3,2,1,0:T(8,128)} %get-tuple-element.23, f32[1,2,4,16,20,128]{5,4,3,2,1,0:T(8,128)S(1)} %get-tuple-element.52, f32[1,2,4,16,20,128]{5,4,3,2,1,0:T(8,128)S(1)} %get-tuple-element.51, ...), kind=kLoop, calls=%fused_computation.77 | loop fusion | flops 10747904 | bytes 27394048 | tf_op jit(solution)/shard_map/add | solution.py:71
  119.0 11.9 %all_to_all.30 = f32[32,1,16]{2,1,0:T(1,128)S(1)} all-to-all(f32[32,1,16]{2,1,0:T(1,128)S(1)} %broadcast_in_dim.8), channel_id=1, replica_groups=mesh['quad'=8,'py'=8,'pz'=4] {'py','pz'}, dimensions={0} | all-to-all | bytes 4096 | tf_op jit(solution)/shard_map/all_to_all | solution.py:34
  131.8 1.1 copy.192
  132.9 7.9 %all-to-all-start.2 = ((f32[1,2,4,16,16,128]{5,4,2,1,0,3:T(8,128)}), f32[1,2,4,16,16,128]{5,4,2,1,0,3:T(8,128)S(1)}, u32[]{:S(2)}, u32[]{:S(2)}) async-start(f32[1,2,4,16,16,128]{5,4,2,1,0,3:T(8,128)} %copy.192), calls=%async_computation.2 | async-start | bytes 2097152 | tf_op jit(solution)/shard_map/all_to_all | solution.py:155
  140.9 31.3 %all-to-all-done.2 = f32[1,2,4,16,16,128]{5,4,2,1,0,3:T(8,128)S(1)} async-done(((f32[1,2,4,16,16,128]{5,4,2,1,0,3:T(8,128)}), f32[1,2,4,16,16,128]{5,4,2,1,0,3:T(8,128)S(1)}, u32[]{:S(2)}, u32[]{:S(2)}) %all-to-all-start.2) | async-done | bytes 1048608 | tf_op jit(solution)/shard_map/all_to_all | solution.py:155
  175.6 0.9 copy.195
  (63 shorter events, 17.0 us)
Async XLA Ops:
  2.5 27.6 %collective-permute-start.1 = (f32[1,2,4,16,4,128]{5,3,4,2,1,0:T(8,128)}, f32[1,2,4,16,4,128]{5,3,4,2,1,0:T(8,128)S(1)}, u32[]{:S(2)}, u32[]{:S(2)}) collective-permute-start(f32[1,2,4,16,4,128]{5,3,4,2,1,0:T(8,128)} %get-tuple-element.79), channel_id=1, source_target_pairs={{0,4},{4,8},{8,12},{12,16},{16,20},{20,24},{24,28},{28,0},{1,5},{5... | collective-permute-start | bytes 786440 | tf_op jit(solution)/shard_map/ppermute | solution.py:20
  4.3 25.8 %collective-permute-start = (f32[1,2,4,16,4,128]{5,3,4,2,1,0:T(8,128)}, f32[1,2,4,16,4,128]{5,3,4,2,1,0:T(8,128)}, u32[]{:S(2)}, u32[]{:S(2)}) collective-permute-start(f32[1,2,4,16,4,128]{5,3,4,2,1,0:T(8,128)} %get-tuple-element.80), channel_id=1, source_target_pairs={{4,0},{8,4},{12,8},{16,12},{20,16},{24,20},{28,24},{0,28},{5,1},{9... | collective-permute-start | bytes 786440 | tf_op jit(solution)/shard_map/ppermute | solution.py:21
  6.3 20.2 %collective-permute-start.2 = (f32[1,2,4,16,16,4]{4,3,5,2,1,0:T(8,128)}, f32[1,2,4,16,16,4]{4,3,5,2,1,0:T(8,128)}, u32[]{:S(2)}, u32[]{:S(2)}) collective-permute-start(f32[1,2,4,16,16,4]{4,3,5,2,1,0:T(8,128)} %copy.158), channel_id=1, source_target_pairs={{1,0},{2,1},{3,2},{0,3},{5,4},{6,5},{7,6},{4,7},{9,8},{10,9},{11,1... | collective-permute-start | bytes 98312 | tf_op jit(solution)/shard_map/ppermute | solution.py:21
  8.3 19.9 %collective-permute-start.3 = (f32[1,2,4,16,16,4]{4,3,5,2,1,0:T(8,128)}, f32[1,2,4,16,16,4]{4,3,5,2,1,0:T(8,128)}, u32[]{:S(2)}, u32[]{:S(2)}) collective-permute-start(f32[1,2,4,16,16,4]{4,3,5,2,1,0:T(8,128)} %copy.160), channel_id=1, source_target_pairs={{0,1},{1,2},{2,3},{3,0},{4,5},{5,6},{6,7},{7,4},{8,9},{9,10},{10,1... | collective-permute-start | bytes 98312 | tf_op jit(solution)/shard_map/ppermute | solution.py:20
  34.8 4.4 %copy-start = (f32[4,16,16,128]{3,2,1,0:T(8,128)S(1)}, f32[4,16,16,128]{3,2,1,0:T(8,128)}, u32[]{:S(2)}) copy-start(f32[4,16,16,128]{3,2,1,0:T(8,128)} %param.5) | copy-start | bytes 1572868
  34.8 4.4 %copy-start.1 = (f32[4,16,16,128]{3,2,1,0:T(8,128)S(1)}, f32[4,16,16,128]{3,2,1,0:T(8,128)}, u32[]{:S(2)}) copy-start(f32[4,16,16,128]{3,2,1,0:T(8,128)} %param.6) | copy-start | bytes 1572868
  34.8 4.4 %copy-start.3 = (f32[16,16,128]{2,1,0:T(8,128)S(1)}, f32[16,16,128]{2,1,0:T(8,128)}, u32[]{:S(2)}) copy-start(f32[16,16,128]{2,1,0:T(8,128)} %param.7) | copy-start | bytes 393220
  50.3 17.3 %all-to-all-start = ((f32[32,1,16]{2,1,0:T(1,128)}), f32[32,1,16]{2,1,0:T(1,128)S(1)}, u32[]{:S(2)}, u32[]{:S(2)}) async-start(f32[32,1,16]{2,1,0:T(1,128)} %broadcast_in_dim.7), calls=%async_computation | async-start | bytes 32768 | tf_op jit(solution)/shard_map/all_to_all | solution.py:34
  76.8 22.3 %collective-permute-start.4 = (f32[1,2,4,16,4,128]{5,3,4,2,1,0:T(8,128)}, f32[1,2,4,16,4,128]{5,3,4,2,1,0:T(8,128)}, u32[]{:S(2)}, u32[]{:S(2)}) collective-permute-start(f32[1,2,4,16,4,128]{5,3,4,2,1,0:T(8,128)} %copy.214), channel_id=1, source_target_pairs={{4,0},{8,4},{12,8},{16,12},{20,16},{24,20},{28,24},{0,28},{5,1},{9... | collective-permute-start | bytes 786440 | tf_op jit(solution)/shard_map/ppermute | solution.py:21
  78.1 22.1 %collective-permute-start.5 = (f32[1,2,4,16,4,128]{5,3,4,2,1,0:T(8,128)}, f32[1,2,4,16,4,128]{5,3,4,2,1,0:T(8,128)}, u32[]{:S(2)}, u32[]{:S(2)}) collective-permute-start(f32[1,2,4,16,4,128]{5,3,4,2,1,0:T(8,128)} %copy.215), channel_id=1, source_target_pairs={{0,4},{4,8},{8,12},{12,16},{16,20},{20,24},{24,28},{28,0},{1,5},{5... | collective-permute-start | bytes 786440 | tf_op jit(solution)/shard_map/ppermute | solution.py:20
  82.1 8.6 %collective-permute-start.6 = (f32[1,2,4,16,16,4]{4,3,5,2,1,0:T(8,128)}, f32[1,2,4,16,16,4]{4,3,5,2,1,0:T(8,128)}, u32[]{:S(2)}, u32[]{:S(2)}) collective-permute-start(f32[1,2,4,16,16,4]{4,3,5,2,1,0:T(8,128)} %copy.216), channel_id=1, source_target_pairs={{1,0},{2,1},{3,2},{0,3},{5,4},{6,5},{7,6},{4,7},{9,8},{10,9},{11,1... | collective-permute-start | bytes 98312 | tf_op jit(solution)/shard_map/ppermute | solution.py:21
  84.8 11.6 %collective-permute-start.7 = (f32[1,2,4,16,16,4]{4,3,5,2,1,0:T(8,128)}, f32[1,2,4,16,16,4]{4,3,5,2,1,0:T(8,128)}, u32[]{:S(2)}, u32[]{:S(2)}) collective-permute-start(f32[1,2,4,16,16,4]{4,3,5,2,1,0:T(8,128)} %copy.217), channel_id=1, source_target_pairs={{0,1},{1,2},{2,3},{3,0},{4,5},{5,6},{6,7},{7,4},{8,9},{9,10},{10,1... | collective-permute-start | bytes 98312 | tf_op jit(solution)/shard_map/ppermute | solution.py:20
  99.1 2.6 %copy-start.2 = (f32[1,2,4,16,16,4]{5,4,3,2,1,0:T(8,128)S(1)}, f32[1,2,4,16,16,4]{5,4,3,2,1,0:T(8,128)}, u32[]{:S(2)}) copy-start(f32[1,2,4,16,16,4]{5,4,3,2,1,0:T(8,128)} %copy.225) | copy-start | bytes 98308
  132.9 39.3 %all-to-all-start.2 = ((f32[1,2,4,16,16,128]{5,4,2,1,0,3:T(8,128)}), f32[1,2,4,16,16,128]{5,4,2,1,0,3:T(8,128)S(1)}, u32[]{:S(2)}, u32[]{:S(2)}) async-start(f32[1,2,4,16,16,128]{5,4,2,1,0,3:T(8,128)} %copy.192), calls=%async_computation.2 | async-start | bytes 2097152 | tf_op jit(solution)/shard_map/all_to_all | solution.py:155
where the time goes:
time: 177 us
  other arithmetic  48.8 us (28%)
  waiting for transfers between devices  43.3 us (24%)
  local copies, waits for them, and re-layouts  42.1 us (24%)
  starting transfers between devices  25.8 us (15%)
  blocking collectives  11.9 us (7%)
  matrix products  2.71 us (2%)
    all_to_all x1, waiting for transfers between devices, per_device(): lax.all_to_all(solution, 'quad', split_axis=3, concat_axis=0, tiled=True)  31.3 us
    add x2, other arithmetic, apply_operator(): return -0.5 * laplace + potential * field  22.7 us
    slice x22, local copies, waits for them, and re-layouts, apply_operator(): beside_all = jnp.roll(field, offset, 3) + jnp.roll(field, -offset, 3)  15.5 us
    unnamed x16, local copies, waits for them, and re-layouts  13.9 us
    concatenate x4, other arithmetic, with_halo(): jnp.concatenate([jnp.pad(low, around), value, jnp.pad(high, around)], axi...  12.3 us
    all_to_all x1, blocking collectives, sent_to_all(): lax.all_to_all(jnp.broadcast_to(value[None], (count, *value.shape)), axis...  11.9 us
    all_to_all x1, starting transfers between devices, sent_to_all(): lax.all_to_all(jnp.broadcast_to(value[None], (count, *value.shape)), axis...  11.2 us
    another operation x10, other arithmetic, per_device(): hres = apply_operator(jnp.stack(residual, 1), potential)  10.1 us
  transfers between devices with their start and end apart: 10, of which 4 were waited for; matrix products, arithmetic and copies ran while one was open for 21% of the time, Pallas kernels for 0%

commit v1 on v0

--- a/solution.py
+++ b/solution.py
@@ -152,7 +152,10 @@
     alpha_next = complex_div(rho_next, curv_next)
     step_part = complex_mul(spread(alpha_next), direction)
     solution = jnp.stack((first_iterate[0] + step_part[0], first_iterate[1] + step_part[1]), 1)
-    gathered = lax.all_to_all(solution, "quad", split_axis=3, concat_axis=0, tiled=True)
+    gathered = jnp.concatenate(
+        lax.all_to_all(jnp.stack(jnp.split(solution, lax.axis_size("quad"), axis=3)), "quad", 0, 0),
+        axis=0,
+    )
     all_angles = 2.0 * math.pi * (jnp.arange(gathered.shape[0]).astype(jnp.float32) + 0.5) / QPTS
     return moment_terms(gathered, all_angles, radius[0])
 

time: 177 us -> 181 us (1.023)
  other arithmetic: 48.8 us -> 54 us
    unnamed x0 -> x7, other arithmetic: none -> 4.6 us
  transfers between devices with their start and end apart: 10 -> 10, of which waited for: 4 -> 4; matrix products, arithmetic and copies ran while one was open for 21% -> 20% of each run, Pallas kernels for 0% -> 0%
where the time goes in v1:
time: 181 us
  other arithmetic  54 us (30%)
  waiting for transfers between devices  43.3 us (24%)
  local copies, waits for them, and re-layouts  41 us (23%)
  starting transfers between devices  25.8 us (14%)
  blocking collectives  11.9 us (7%)
  matrix products  2.71 us (1%)
    all_to_all x1, waiting for transfers between devices, per_device(): lax.all_to_all(jnp.stack(jnp.split(solution, lax.axis_size('quad'), axis=...  31.3 us
    add x2, other arithmetic, apply_operator(): return -0.5 * laplace + potential * field  22.7 us
    slice x22, local copies, waits for them, and re-layouts, apply_operator(): beside_all = jnp.roll(field, offset, 3) + jnp.roll(field, -offset, 3)  15.5 us
    unnamed x16, local copies, waits for them, and re-layouts  13.9 us
    concatenate x4, other arithmetic, with_halo(): jnp.concatenate([jnp.pad(low, around), value, jnp.pad(high, around)], axi...  12.3 us
    all_to_all x1, blocking collectives, sent_to_all(): lax.all_to_all(jnp.broadcast_to(value[None], (count, *value.shape)), axis...  11.9 us
    all_to_all x1, starting transfers between devices, sent_to_all(): lax.all_to_all(jnp.broadcast_to(value[None], (count, *value.shape)), axis...  11.2 us
    another operation x10, other arithmetic, per_device(): hres = apply_operator(jnp.stack(residual, 1), potential)  10.1 us
  transfers between devices with their start and end apart: 10, of which 4 were waited for; matrix products, arithmetic and copies ran while one was open for 20% of the time, Pallas kernels for 0%

profile of v1, /device:TPU:33, one launch (start us, length us, event | category | flops | bytes accessed | tf_op | source)
XLA Modules:
  0.0 180.6 jit_solution(8539376305006599491)
XLA Ops:
  0.0 1.3 pad_maximum_fusion.5
  1.6 0.9 fusion.112
  2.5 1.9 %collective-permute-start.1 = (f32[1,2,4,16,4,128]{5,3,4,2,1,0:T(8,128)}, f32[1,2,4,16,4,128]{5,3,4,2,1,0:T(8,128)S(1)}, u32[]{:S(2)}, u32[]{:S(2)}) collective-permute-start(f32[1,2,4,16,4,128]{5,3,4,2,1,0:T(8,128)} %get-tuple-element.79), channel_id=1, source_target_pairs={{0,4},{4,8},{8,12},{12,16},{16,20},{20,24},{24,28},{28,0},{1,5},{5... | collective-permute-start | bytes 786440 | tf_op jit(solution)/shard_map/ppermute | solution.py:20
  4.7 1.6 copy.158
  6.7 1.6 copy.160
  8.3 1.3 collective-permute-start.3
  10.7 0.7 fusion.110
  11.4 1.3 copy.156
  12.7 1.3 copy.150
  14.0 1.2 copy.151
  15.3 1.2 copy.163
  16.5 1.2 copy.164
  17.7 1.2 copy.169
  18.9 1.2 copy.170
  20.1 1.1 copy.175
  21.2 1.1 copy.176
  26.5 1.8 copy.218
  28.3 1.8 copy.219
  30.1 1.1 copy.157
  31.2 3.6 %select_maximum_fusion.3 = (f32[1,2,4,16,24,132]{5,4,3,2,1,0:T(8,128)S(1)}, f32[1,2,4,16,24,132]{5,4,3,2,1,0:T(8,128)S(1)}) fusion(f32[1,2,4,16,16,4]{5,4,3,2,1,0:T(8,128)S(1)} %copy.218, f32[1,2,4,16,4,128]{5,4,3,2,1,0:T(4,128)S(1)} %copy.157, f32[1,2,4,16,16,128]{5,4,3,2,1,0:T(8,128)} %copy.156, f32[1,2,4,16,4,128]{5,4,3,2,1,0:T(4,128)S(1)} %copy.155, ...), kind=kLoop, calls=%fused_computation.45 | loop fusion | flops 4055040 | bytes 4882432 | tf_op jit(solution)/shard_map/concatenate | solution.py:27
  34.8 4.4 %fusion.6 = (f32[1,2,4,16,16,128]{5,3,4,2,1,0:T(8,128)}, f32[1,2,4,16,16,128]{5,3,4,2,1,0:T(8,128)}, f32[1,2,4,16,16,128]{5,3,4,2,1,0:T(8,128)}, f32[1,2,4,16,16...) fusion(f32[1,2,4,16,16,128]{5,3,4,2,1,0:T(8,128)S(1)} %bitcast., ...), kind=kLoop, calls=%fused_computation.83 | loop fusion | flops 2097152 | bytes 9961472 | tf_op jit(solution)/shard_map/concatenate | solution.py:27
  39.2 10.0 %fusion.23 = f32[1,2,4,16,16,128]{5,4,3,2,1,0:T(8,128)S(1)} fusion(f32[1,2,4,16,24,132]{5,4,3,2,1,0:T(8,128)S(1)} %get-tuple-element.26, f32[1,2,4,16,24,132]{5,4,3,2,1,0:T(8,128)S(1)} %get-tuple-element.25, f32[1,2,4,15,16,128]{5,4,3,2,1,0:T(8,128)} %copy.150, f32[1,2,4,1,16,128]{5,4,3,2,1,0:T(8,128)} %bitcast.166, f32[1,2,4,1,16,128]{5,4,3,2,1,0:T(8,128)} %bitcast.165, ...), kind=kLoop, calls=%fused_computation.117 | loop fusion | flops 10747904 | bytes 27394048 | tf_op jit(solution)/shard_map/add | solution.py:71
  50.3 11.2 %all-to-all-start = ((f32[32,1,16]{2,1,0:T(1,128)}), f32[32,1,16]{2,1,0:T(1,128)S(1)}, u32[]{:S(2)}, u32[]{:S(2)}) async-start(f32[32,1,16]{2,1,0:T(1,128)} %broadcast_in_dim.7), calls=%async_computation | async-start | bytes 32768 | tf_op jit(solution)/shard_map/all_to_all | solution.py:34
  63.0 4.6 %all-to-all-done = f32[32,1,16]{2,1,0:T(1,128)S(1)} async-done(((f32[32,1,16]{2,1,0:T(1,128)}), f32[32,1,16]{2,1,0:T(1,128)S(1)}, u32[]{:S(2)}, u32[]{:S(2)}) %all-to-all-start) | async-done | bytes 2080 | tf_op jit(solution)/shard_map/all_to_all | solution.py:34
  68.0 0.7 fusion.53
  68.8 0.8 fusion.55
  69.6 1.3 fusion.43
  71.6 1.5 fusion.41
  73.1 1.5 fusion.39
  74.7 1.3 fusion.8
  76.1 0.7 copy.210
  78.1 1.1 collective-permute-start.5
  79.3 2.8 %copy.212 = f32[1,2,4,16,16,4]{4,3,5,2,1,0:T(8,128)} copy(f32[1,2,4,16,16,4]{5,4,3,2,1,0:T(8,128)} %get-tuple-element.53) | data formatting | bytes 65536
  82.1 1.1 collective-permute-start.6
  83.2 1.6 copy.213
  85.1 1.4 fusion.45
  87.2 3.6 %collective-permute-done.6 = f32[1,2,4,16,16,4]{4,3,5,2,1,0:T(8,128)} collective-permute-done((f32[1,2,4,16,16,4]{4,3,5,2,1,0:T(8,128)}, f32[1,2,4,16,16,4]{4,3,5,2,1,0:T(8,128)}, u32[]{:S(2)}, u32[]{:S(2)}) %collective-permute-start.6) | collective-permute-done | bytes 32800 | tf_op jit(solution)/shard_map/ppermute | solution.py:21
  90.7 1.8 copy.220
  92.5 3.9 %collective-permute-done.7 = f32[1,2,4,16,16,4]{4,3,5,2,1,0:T(8,128)} collective-permute-done((f32[1,2,4,16,16,4]{4,3,5,2,1,0:T(8,128)}, f32[1,2,4,16,16,4]{4,3,5,2,1,0:T(8,128)}, u32[]{:S(2)}, u32[]{:S(2)}) %collective-permute-start.7) | collective-permute-done | bytes 32800 | tf_op jit(solution)/shard_map/ppermute | solution.py:20
  96.4 2.7 %copy.221 = f32[1,2,4,16,16,4]{5,4,3,2,1,0:T(8,128)} copy(f32[1,2,4,16,16,4]{4,3,5,2,1,0:T(8,128)} %collective-permute-done.7) | data formatting | bytes 65536
  99.1 1.1 copy.182
  100.3 1.1 copy.184
  101.7 4.0 %select_maximum_fusion.1 = (f32[1,2,4,16,24,132]{5,4,3,2,1,0:T(8,128)}, f32[1,2,4,16,24,132]{5,4,3,2,1,0:T(8,128)}) fusion(f32[1,2,4,16,16,4]{5,4,3,2,1,0:T(8,128)S(1)} %copy.220, f32[1,2,4,16,4,128]{5,4,3,2,1,0:T(4,128)S(1)} %copy.182, f32[1,1,4,16,16,128]{5,4,3,2,1,0:T(8,128)S(1)} %bitcast.155, f32[1,1,4,16,16,128]{5,4,3,2,1,0:T(8,128)S(1)} %bitcast.142, ...), kind=kLoop, calls=%fused_computation.42 | loop fusion | flops 4866048 | bytes 4882432 | tf_op jit(solution)/shard_map/concatenate | solution.py:27
  105.7 12.7 %fusion.13 = f32[1,2,4,16,16,128]{5,4,3,2,1,0:T(8,128)S(1)} fusion(f32[1,2,4,16,24,132]{5,4,3,2,1,0:T(8,128)} %get-tuple-element.24, f32[1,2,4,16,24,132]{5,4,3,2,1,0:T(8,128)} %get-tuple-element.23, f32[1,2,4,16,20,128]{5,4,3,2,1,0:T(8,128)S(1)} %get-tuple-element.52, f32[1,2,4,16,20,128]{5,4,3,2,1,0:T(8,128)S(1)} %get-tuple-element.51, ...), kind=kLoop, calls=%fused_computation.91 | loop fusion | flops 10747904 | bytes 27394048 | tf_op jit(solution)/shard_map/add | solution.py:71
  119.0 11.9 %all_to_all.17 = f32[32,1,16]{2,1,0:T(1,128)S(1)} all-to-all(f32[32,1,16]{2,1,0:T(1,128)S(1)} %broadcast_in_dim.8), channel_id=1, replica_groups=mesh['quad'=8,'py'=8,'pz'=4] {'py','pz'}, dimensions={0} | all-to-all | bytes 4096 | tf_op jit(solution)/shard_map/all_to_all | solution.py:34
  137.0 7.9 %all-to-all-start.2 = ((f32[8,1,2,4,2,16,128]{6,5,4,3,2,1,0:T(8,128)}), f32[8,1,2,4,2,16,128]{6,5,4,3,2,1,0:T(8,128)S(1)}, u32[]{:S(2)}, u32[]{:S(2)}) async-start(f32[8,1,2,4,2,16,128]{6,5,4,3,2,1,0:T(8,128)} %fusion.80), calls=%async_computation.2 | async-start | bytes 2097152 | tf_op jit(solution)/shard_map/all_to_all | solution.py:156
  144.9 31.3 %all-to-all-done.2 = f32[8,1,2,4,2,16,128]{6,5,4,3,2,1,0:T(8,128)S(1)} async-done(((f32[8,1,2,4,2,16,128]{6,5,4,3,2,1,0:T(8,128)}), f32[8,1,2,4,2,16,128]{6,5,4,3,2,1,0:T(8,128)S(1)}, u32[]{:S(2)}, u32[]{:S(2)}) %all-to-all-start.2) | async-done | bytes 1048608 | tf_op jit(solution)/shard_map/all_to_all | solution.py:156
  179.7 0.9 copy.193
  (69 shorter events, 21.5 us)
Async XLA Ops:
  2.5 27.6 %collective-permute-start.1 = (f32[1,2,4,16,4,128]{5,3,4,2,1,0:T(8,128)}, f32[1,2,4,16,4,128]{5,3,4,2,1,0:T(8,128)S(1)}, u32[]{:S(2)}, u32[]{:S(2)}) collective-permute-start(f32[1,2,4,16,4,128]{5,3,4,2,1,0:T(8,128)} %get-tuple-element.79), channel_id=1, source_target_pairs={{0,4},{4,8},{8,12},{12,16},{16,20},{20,24},{24,28},{28,0},{1,5},{5... | collective-permute-start | bytes 786440 | tf_op jit(solution)/shard_map/ppermute | solution.py:20
  4.3 25.8 %collective-permute-start = (f32[1,2,4,16,4,128]{5,3,4,2,1,0:T(8,128)}, f32[1,2,4,16,4,128]{5,3,4,2,1,0:T(8,128)}, u32[]{:S(2)}, u32[]{:S(2)}) collective-permute-start(f32[1,2,4,16,4,128]{5,3,4,2,1,0:T(8,128)} %get-tuple-element.80), channel_id=1, source_target_pairs={{4,0},{8,4},{12,8},{16,12},{20,16},{24,20},{28,24},{0,28},{5,1},{9... | collective-permute-start | bytes 786440 | tf_op jit(solution)/shard_map/ppermute | solution.py:21
  6.3 20.2 %collective-permute-start.2 = (f32[1,2,4,16,16,4]{4,3,5,2,1,0:T(8,128)}, f32[1,2,4,16,16,4]{4,3,5,2,1,0:T(8,128)}, u32[]{:S(2)}, u32[]{:S(2)}) collective-permute-start(f32[1,2,4,16,16,4]{4,3,5,2,1,0:T(8,128)} %copy.158), channel_id=1, source_target_pairs={{1,0},{2,1},{3,2},{0,3},{5,4},{6,5},{7,6},{4,7},{9,8},{10,9},{11,1... | collective-permute-start | bytes 98312 | tf_op jit(solution)/shard_map/ppermute | solution.py:21
  8.3 19.9 %collective-permute-start.3 = (f32[1,2,4,16,16,4]{4,3,5,2,1,0:T(8,128)}, f32[1,2,4,16,16,4]{4,3,5,2,1,0:T(8,128)}, u32[]{:S(2)}, u32[]{:S(2)}) collective-permute-start(f32[1,2,4,16,16,4]{4,3,5,2,1,0:T(8,128)} %copy.160), channel_id=1, source_target_pairs={{0,1},{1,2},{2,3},{3,0},{4,5},{5,6},{6,7},{7,4},{8,9},{9,10},{10,1... | collective-permute-start | bytes 98312 | tf_op jit(solution)/shard_map/ppermute | solution.py:20
  34.8 4.4 %copy-start = (f32[4,16,16,128]{3,2,1,0:T(8,128)S(1)}, f32[4,16,16,128]{3,2,1,0:T(8,128)}, u32[]{:S(2)}) copy-start(f32[4,16,16,128]{3,2,1,0:T(8,128)} %param.5) | copy-start | bytes 1572868
  34.8 4.4 %copy-start.1 = (f32[4,16,16,128]{3,2,1,0:T(8,128)S(1)}, f32[4,16,16,128]{3,2,1,0:T(8,128)}, u32[]{:S(2)}) copy-start(f32[4,16,16,128]{3,2,1,0:T(8,128)} %param.6) | copy-start | bytes 1572868
  34.8 4.4 %copy-start.3 = (f32[16,16,128]{2,1,0:T(8,128)S(1)}, f32[16,16,128]{2,1,0:T(8,128)}, u32[]{:S(2)}) copy-start(f32[16,16,128]{2,1,0:T(8,128)} %param.7) | copy-start | bytes 393220
  50.3 17.3 %all-to-all-start = ((f32[32,1,16]{2,1,0:T(1,128)}), f32[32,1,16]{2,1,0:T(1,128)S(1)}, u32[]{:S(2)}, u32[]{:S(2)}) async-start(f32[32,1,16]{2,1,0:T(1,128)} %broadcast_in_dim.7), calls=%async_computation | async-start | bytes 32768 | tf_op jit(solution)/shard_map/all_to_all | solution.py:34
  76.8 22.3 %collective-permute-start.4 = (f32[1,2,4,16,4,128]{5,3,4,2,1,0:T(8,128)}, f32[1,2,4,16,4,128]{5,3,4,2,1,0:T(8,128)}, u32[]{:S(2)}, u32[]{:S(2)}) collective-permute-start(f32[1,2,4,16,4,128]{5,3,4,2,1,0:T(8,128)} %copy.210), channel_id=1, source_target_pairs={{4,0},{8,4},{12,8},{16,12},{20,16},{24,20},{28,24},{0,28},{5,1},{9... | collective-permute-start | bytes 786440 | tf_op jit(solution)/shard_map/ppermute | solution.py:21
  78.1 22.1 %collective-permute-start.5 = (f32[1,2,4,16,4,128]{5,3,4,2,1,0:T(8,128)}, f32[1,2,4,16,4,128]{5,3,4,2,1,0:T(8,128)}, u32[]{:S(2)}, u32[]{:S(2)}) collective-permute-start(f32[1,2,4,16,4,128]{5,3,4,2,1,0:T(8,128)} %copy.211), channel_id=1, source_target_pairs={{0,4},{4,8},{8,12},{12,16},{16,20},{20,24},{24,28},{28,0},{1,5},{5... | collective-permute-start | bytes 786440 | tf_op jit(solution)/shard_map/ppermute | solution.py:20
  82.1 8.6 %collective-permute-start.6 = (f32[1,2,4,16,16,4]{4,3,5,2,1,0:T(8,128)}, f32[1,2,4,16,16,4]{4,3,5,2,1,0:T(8,128)}, u32[]{:S(2)}, u32[]{:S(2)}) collective-permute-start(f32[1,2,4,16,16,4]{4,3,5,2,1,0:T(8,128)} %copy.212), channel_id=1, source_target_pairs={{1,0},{2,1},{3,2},{0,3},{5,4},{6,5},{7,6},{4,7},{9,8},{10,9},{11,1... | collective-permute-start | bytes 98312 | tf_op jit(solution)/shard_map/ppermute | solution.py:21
  84.8 11.6 %collective-permute-start.7 = (f32[1,2,4,16,16,4]{4,3,5,2,1,0:T(8,128)}, f32[1,2,4,16,16,4]{4,3,5,2,1,0:T(8,128)}, u32[]{:S(2)}, u32[]{:S(2)}) collective-permute-start(f32[1,2,4,16,16,4]{4,3,5,2,1,0:T(8,128)} %copy.213), channel_id=1, source_target_pairs={{0,1},{1,2},{2,3},{3,0},{4,5},{5,6},{6,7},{7,4},{8,9},{9,10},{10,1... | collective-permute-start | bytes 98312 | tf_op jit(solution)/shard_map/ppermute | solution.py:20
  99.1 2.6 %copy-start.2 = (f32[1,2,4,16,16,4]{5,4,3,2,1,0:T(8,128)S(1)}, f32[1,2,4,16,16,4]{5,4,3,2,1,0:T(8,128)}, u32[]{:S(2)}) copy-start(f32[1,2,4,16,16,4]{5,4,3,2,1,0:T(8,128)} %copy.221) | copy-start | bytes 98308
  137.0 39.3 %all-to-all-start.2 = ((f32[8,1,2,4,2,16,128]{6,5,4,3,2,1,0:T(8,128)}), f32[8,1,2,4,2,16,128]{6,5,4,3,2,1,0:T(8,128)S(1)}, u32[]{:S(2)}, u32[]{:S(2)}) async-start(f32[8,1,2,4,2,16,128]{6,5,4,3,2,1,0:T(8,128)} %fusion.80), calls=%async_computation.2 | async-start | bytes 2097152 | tf_op jit(solution)/shard_map/all_to_all | solution.py:156
